TPU v7x, 32 devices: a whole 2x2x4 slice. The times are simulated.
32 devices in a mesh: groups: 2 (over y), blocks: 4 (over z), pairs: 2 (over x), sub: 2 (over core).
Axes of the slice: x: 2, y: 2, z: 4, core: 2. Of those that a mesh axis runs over, the one named last changes fastest.
Arguments:
- coords: float32 [3, 131072], P(None, ('groups', 'blocks')), parts along dimension 1, may hold values from 0 to 132, as said below
- probes: float32 [8, 131072], P(None, ('groups', 'blocks')), parts along dimension 1, may hold values from -6 to 6
- noise: float32 [131072], P(('groups', 'blocks')), parts along dimension 0, may hold values from 0.2 to 1
- pair_list: int32 [2, 6144], P(None, ('groups', 'blocks', 'pairs', 'sub')), parts along dimension 1, may hold values from 0 to 255, as said below
- pair_count: int32 [32], P(('groups', 'blocks', 'pairs', 'sub')), parts along dimension 0, may hold values from 1 to 192
- coeffs: float32 [10], P('groups'), parts along dimension 0, may hold values from 0.5 to 1.5
Outputs:
- poly_probes: float32 [8, 131072], P(None, ('groups', 'blocks')), parts along dimension 1
There are 2 independent parts, one for each index of `groups`. A program takes and returns all parts, laid end to end along the dimension named above; each array names one. Nothing has to cross between parts.
Inputs may be any that keep to these rules, and one draw needn't show every extreme that they name: `pair_list`: the list of slot s belongs to index b = s // 768 of blocks; its first block i lies in b * 64 to (b + 1) * 64 - 1, and i <= j < i + 8. Slots past the count hold pairs too, which are not used. A pair may be listed more than once; each live listing counts. `coords`: rows x, y, z. The points of block k lie within x from k / 2 to k / 2 + 3.5, and y, z from 0 to 3.
All inputs are finite; a program needn't handle non-finite values.
Results may differ from a plain program's by a relative error of at most 0.00019.
Values sent between devices are 32-bit elements; how exact they have to be, the bound alone decides.
A program may use at most 192 MiB of HBM per device.

v0:
```python
import math

import jax
import jax.numpy as jnp
from jax import lax
from jax.sharding import PartitionSpec as P

PTS_BLK = 256
REACH = 8
DEG = 4


kernel_scale = 0.1
spectrum_center = 1.0
spectrum_half = 2.0


def shifted(value, axis, steps):
    count = lax.axis_size(axis)
    leading, last = (max(0, -steps), min(count, count - steps))
    return lax.ppermute(value, axis, [(source, source + steps) for source in range(leading, last)])


def wendland(first, second):
    diff = first[:, :, :, None] - second[:, :, None, :]
    dist = jnp.sqrt(jnp.sum(diff * diff, axis=0))
    inside = jnp.maximum(1.0 - dist, 0.0)
    return kernel_scale * inside**4 * (4.0 * dist + 1.0)


def on_device(coords, probes, noise, pair_list, pair_count, coeffs):
    probe_count, local_pts = probes.shape
    blocks_here = local_pts // PTS_BLK
    rim_pts = REACH * PTS_BLK
    ext_blocks = blocks_here + REACH
    pair_cap = pair_list.shape[1]
    first_block = lax.axis_index("blocks") * blocks_here
    coords_next = shifted(coords[:, :rim_pts], "blocks", -1)
    coords_ext = jnp.concatenate([coords, coords_next], 1).reshape(3, ext_blocks, PTS_BLK)
    rows_here = pair_list[0] - first_block
    cols_here = pair_list[1] - first_block
    live = jnp.arange(pair_cap, dtype=jnp.int32) < pair_count[0]
    reverse = live & (rows_here != cols_here)
    column_ids = jnp.arange(ext_blocks, dtype=jnp.int32)
    onehot_rows = ((rows_here[:, None] == column_ids[None, :]) & live[:, None]).astype(jnp.float32)
    onehot_cols = ((cols_here[:, None] == column_ids[None, :]) & reverse[:, None]).astype(
        jnp.float32
    )
    group = math.gcd(pair_cap, 8)
    turns = pair_cap // group

    def build_tiles(item):
        row_ids, col_ids = item
        return wendland(
            jnp.take(coords_ext, row_ids, axis=1), jnp.take(coords_ext, col_ids, axis=1)
        )

    tiles = lax.map(build_tiles, (rows_here.reshape(turns, group), cols_here.reshape(turns, group)))
    tiles = tiles.reshape(pair_cap, PTS_BLK, PTS_BLK)

    def pair_terms(extended):
        fwd = jnp.einsum(
            "gab,qgb->gqa",
            tiles,
            jnp.take(extended, cols_here, axis=1),
            precision=lax.Precision.HIGHEST,
        )
        bwd = jnp.einsum(
            "gab,qga->gqb",
            tiles,
            jnp.take(extended, rows_here, axis=1),
            precision=lax.Precision.HIGHEST,
        )
        acc = jnp.einsum("gk,gqa->qka", onehot_rows, fwd, precision=lax.Precision.HIGHEST)
        acc = acc + jnp.einsum("gk,gqa->qka", onehot_cols, bwd, precision=lax.Precision.HIGHEST)
        return acc.reshape(probe_count, ext_blocks * PTS_BLK)

    def apply_kernel(vec):
        rim_in = shifted(vec[:, :rim_pts], "blocks", -1)
        extended = jnp.concatenate([vec, rim_in], 1).reshape(probe_count, ext_blocks, PTS_BLK)
        terms = pair_terms(extended)
        arrived = shifted(terms[:, local_pts:], "blocks", 1)
        own_terms = terms[:, :local_pts] + jnp.pad(arrived, ((0, 0), (0, local_pts - rim_pts)))
        total = lax.psum(own_terms, ("pairs", "sub"))
        return noise[None, :] * vec + total

    def scaled(vec):
        return (apply_kernel(vec) - spectrum_center * vec) / spectrum_half

    previous = probes
    current = scaled(probes)
    result = coeffs[0] * previous + coeffs[1] * current
    for order in range(2, DEG + 1):
        following = 2.0 * scaled(current) - previous
        result = result + coeffs[order] * following
        previous = current
        current = following
    return result


def solution(mesh):
    return jax.shard_map(
        on_device,
        mesh=mesh,
        in_specs=(
            P(None, ("groups", "blocks")),
            P(None, ("groups", "blocks")),
            P(("groups", "blocks")),
            P(None, ("groups", "blocks", "pairs", "sub")),
            P(("groups", "blocks", "pairs", "sub")),
            P("groups"),
        ),
        out_specs=P(None, ("groups", "blocks")),
        check_vma=False,
    )
```

profile of v0, /device:TPU:0, one launch (start us, length us, event | category | flops | bytes accessed | tf_op | source)
XLA Modules:
  0.0 678.6 jit_solution(3559572570175304746)
XLA Ops:
  15.1 116.9 %while.10 = (s32[]{:T(128)}, f32[24,8,256,256]{3,2,1,0:T(8,128)}, s32[24,8]{1,0:T(8,128)S(1)}, f32[3,72,256]{2,0,1:T(4,128)S(1)}, s32[24,8]{1,0:T(8,128)S(1)}, /*index=5*/s32[]{:T(128)}) while((s32[]{:T(128)}, f32[24,8,256,256]{3,2,1,0:T(8,128)}, s32[24,8]{1,0:T(8,128)S(1)}, f32[3,72,256]{2,0,1:T(4,128)S(1)}, s32[24,8]{1,0:T(8,128)S(1)}, ...), condition=%wide.region_2.0_spmd, body=%wide.region_0.4_spmd.sunk | while | flops 8403042 | bytes 6644085 | solution.py:58
  76.1 2.4 bitcast_dynamic-update-slice_fusion.2
  100.4 2.4 bitcast_dynamic-update-slice_fusion.2
  115.0 2.4 bitcast_dynamic-update-slice_fusion.2
  135.0 31.3 %fusion.14 = f32[192,8,256]{2,1,0:T(8,128)} fusion(f32[192,256,256]{2,1,0:T(8,128)} %bitcast.98, f32[192,8,256]{2,1,0:T(8,128)} %gather_fusion.3, pred[192]{0:T(512)(128)(4,1)S(1)} %get-tuple-element.59), kind=kOutput, calls=%fused_computation.36 | convolution fusion | flops 1208352768 | bytes 53477568 | tf_op jit(solution)/shard_map/gab,qga->gqb/dot_general | solution.py:68
  166.3 2.5 fusion.30
  168.8 47.8 %fusion.16 = f32[192,8,256]{2,1,0:T(8,128)} fusion(f32[192,256,256]{2,1,0:T(8,128)} %bitcast.99, f32[192,8,256]{2,1,0:T(8,128)S(1)} %gather_fusion.2, pred[192]{0:T(512)(128)(4,1)S(1)} %get-tuple-element.57), kind=kOutput, calls=%fused_computation.38 | convolution fusion | flops 1208352768 | bytes 53477568 | tf_op jit(solution)/shard_map/gab,qgb->gqa/dot_general | solution.py:62
  216.6 2.5 fusion.63
  219.3 5.7 collective-permute-start.2
  227.8 36.2 %all-reduce.9.cloned.1.call-done = f32[8,16384]{1,0:T(8,128)} async-done(((f32[8,16384]{1,0:T(8,128)}), f32[8,16384]{1,0:T(8,128)}) %all-reduce.9.cloned.1.call-update) | async-done | bytes 524304 | tf_op jit(solution)/shard_map/psum | solution.py:84
  266.5 4.9 collective-permute-done.3
  274.3 30.8 %fusion.10 = f32[192,8,256]{2,1,0:T(8,128)} fusion(f32[192,256,256]{2,1,0:T(8,128)} %bitcast.100, f32[192,8,256]{2,1,0:T(8,128)} %gather_fusion.5, pred[192]{0:T(512)(128)(4,1)S(1)} %get-tuple-element.59), kind=kOutput, calls=%fused_computation.32 | convolution fusion | flops 1208352768 | bytes 53477568 | tf_op jit(solution)/shard_map/gab,qga->gqb/dot_general | solution.py:68
  305.2 2.5 fusion.26
  307.7 47.8 %fusion.12 = f32[192,8,256]{2,1,0:T(8,128)} fusion(f32[192,256,256]{2,1,0:T(8,128)} %bitcast.101, f32[192,8,256]{2,1,0:T(8,128)S(1)} %gather_fusion.4, pred[192]{0:T(512)(128)(4,1)S(1)} %get-tuple-element.57), kind=kOutput, calls=%fused_computation.34 | convolution fusion | flops 1208352768 | bytes 53477568 | tf_op jit(solution)/shard_map/gab,qgb->gqa/dot_general | solution.py:62
  355.5 2.5 fusion.60
  358.2 3.4 collective-permute-start.4
  364.8 32.8 %all-reduce.11.cloned.1.call-done = f32[8,16384]{1,0:T(8,128)} async-done(((f32[8,16384]{1,0:T(8,128)}), f32[8,16384]{1,0:T(8,128)}) %all-reduce.11.cloned.1.call-update) | async-done | bytes 524304 | tf_op jit(solution)/shard_map/psum | solution.py:84
  400.1 4.9 collective-permute-done.5
  408.0 30.9 %fusion.6 = f32[192,8,256]{2,1,0:T(8,128)} fusion(f32[192,256,256]{2,1,0:T(8,128)} %bitcast.102, f32[192,8,256]{2,1,0:T(8,128)} %gather_fusion.7, pred[192]{0:T(512)(128)(4,1)S(1)} %get-tuple-element.59), kind=kOutput, calls=%fused_computation.28 | convolution fusion | flops 1208352768 | bytes 53477568 | tf_op jit(solution)/shard_map/gab,qga->gqb/dot_general | solution.py:68
  438.9 3.3 fusion.22
  442.2 47.8 %fusion.8 = f32[192,8,256]{2,1,0:T(8,128)} fusion(f32[192,256,256]{2,1,0:T(8,128)} %bitcast.103, f32[192,8,256]{2,1,0:T(8,128)S(1)} %gather_fusion.6, pred[192]{0:T(512)(128)(4,1)S(1)} %get-tuple-element.57), kind=kOutput, calls=%fused_computation.30 | convolution fusion | flops 1208352768 | bytes 53477568 | tf_op jit(solution)/shard_map/gab,qgb->gqa/dot_general | solution.py:62
  489.9 2.6 fusion.57
  492.8 3.4 collective-permute-start.6
  499.2 33.0 %all-reduce.13.cloned.1.call-done = f32[8,16384]{1,0:T(8,128)} async-done(((f32[8,16384]{1,0:T(8,128)}), f32[8,16384]{1,0:T(8,128)}) %all-reduce.13.cloned.1.call-update) | async-done | bytes 524304 | tf_op jit(solution)/shard_map/psum | solution.py:84
  534.7 4.9 collective-permute-done.7
  542.5 30.9 %fusion.2 = f32[192,8,256]{2,1,0:T(8,128)} fusion(f32[192,256,256]{2,1,0:T(8,128)} %bitcast.104, f32[192,8,256]{2,1,0:T(8,128)} %gather_fusion.9, pred[192]{0:T(512)(128)(4,1)S(1)} %get-tuple-element.59), kind=kOutput, calls=%fused_computation.24 | convolution fusion | flops 1208352768 | bytes 53477568 | tf_op jit(solution)/shard_map/gab,qga->gqb/dot_general | solution.py:68
  573.4 3.3 fusion.18
  576.7 47.8 %fusion.4 = f32[192,8,256]{2,1,0:T(8,128)} fusion(f32[192,256,256]{2,1,0:T(8,128)} %bitcast.105, f32[192,8,256]{2,1,0:T(8,128)S(1)} %gather_fusion.8, pred[192]{0:T(512)(128)(4,1)S(1)} %get-tuple-element.57), kind=kOutput, calls=%fused_computation.26 | convolution fusion | flops 1208352768 | bytes 53477568 | tf_op jit(solution)/shard_map/gab,qgb->gqa/dot_general | solution.py:62
  624.6 2.6 fusion.54
  627.5 3.5 collective-permute-start.8
  635.1 32.0 %all-reduce.15.cloned.1.call-done = f32[8,16384]{1,0:T(8,128)} async-done(((f32[8,16384]{1,0:T(8,128)}), f32[8,16384]{1,0:T(8,128)}) %all-reduce.15.cloned.1.call-update) | async-done | bytes 524304 | tf_op jit(solution)/shard_map/psum | solution.py:84
  667.0 4.7 multiply_add_fusion
  (340 shorter events, 149.0 us)
Async XLA Ops:
  6.5 257.5 %all-reduce.9.cloned.1.call-start = ((), (), s32[]{:S(2)}) async-start(), calls=%async_computation | async-start | bytes 1048576 | tf_op jit(solution)/shard_map/psum | solution.py:84
  7.3 6.8 %collective-permute-start.1 = (f32[3,2048]{1,0:T(4,128)S(1)}, f32[3,2048]{1,0:T(4,128)S(1)}, u32[]{:S(2)}, u32[]{:S(2)}) collective-permute-start(f32[3,2048]{1,0:T(4,128)S(1)} %slice.64), channel_id=1, source_target_pairs={{4,0},{8,4},{12,8},{5,1},{9,5},{13,9},{6,2},{10,6},{14,10},{7,3},{... | collective-permute-start | bytes 73736 | tf_op jit(solution)/shard_map/ppermute | solution.py:21
  9.4 122.6 %collective-permute-start = (f32[8,2048]{1,0:T(8,128)S(1)}, f32[8,2048]{1,0:T(8,128)S(1)}, u32[]{:S(2)}, u32[]{:S(2)}) collective-permute-start(f32[8,2048]{1,0:T(8,128)S(1)} %slice.61), channel_id=1, source_target_pairs={{4,0},{8,4},{12,8},{5,1},{9,5},{13,9},{6,2},{10,6},{14,10},{7,3},{... | collective-permute-start | bytes 196616 | tf_op jit(solution)/shard_map/ppermute | solution.py:21
  15.1 116.9 %copy-start = (f32[8,16384]{1,0:T(8,128)S(1)}, f32[8,16384]{1,0:T(8,128)}, u32[]{:S(2)}) copy-start(f32[8,16384]{1,0:T(8,128)} %param.13) | copy-start | bytes 1572868
  219.1 44.9 %copy-start.5 = (f32[16384]{0:T(1024)S(1)}, f32[16384]{0:T(1024)}, u32[]{:S(2)}) copy-start(f32[16384]{0:T(1024)} %param.14) | copy-start | bytes 196612
  219.3 7.6 %collective-permute-start.2 = (f32[8,2048]{1,0:T(8,128)S(1)}, f32[8,2048]{1,0:T(8,128)S(1)}, u32[]{:S(2)}, u32[]{:S(2)}) collective-permute-start(f32[8,2048]{1,0:T(8,128)S(1)} %slice.101), channel_id=1, source_target_pairs={{0,4},{4,8},{8,12},{1,5},{5,9},{9,13},{2,6},{6,10},{10,14},{3,7},{... | collective-permute-start | bytes 196616 | tf_op jit(solution)/shard_map/ppermute | solution.py:21
  227.8 169.9 %all-reduce.11.cloned.1.call-start = ((), (), s32[]{:S(2)}) async-start(), calls=%async_computation.1 | async-start | bytes 1048576 | tf_op jit(solution)/shard_map/psum | solution.py:84
  265.2 6.2 collective-permute-start.3
  358.0 39.6 %copy-start.1 = (f32[8,16384]{1,0:T(8,128)S(1)}, f32[8,16384]{1,0:T(8,128)}, u32[]{:S(2)}) copy-start(f32[8,16384]{1,0:T(8,128)} %all-reduce.9.cloned.1.call-done) | copy-start | bytes 1572868
  358.2 5.3 collective-permute-start.4
  364.4 167.8 %all-reduce.13.cloned.1.call-start = ((), (), s32[]{:S(2)}) async-start(), calls=%async_computation.2 | async-start | bytes 1048576 | tf_op jit(solution)/shard_map/psum | solution.py:84
  398.8 6.2 collective-permute-start.5
  492.6 39.6 %copy-start.2 = (f32[8,16384]{1,0:T(8,128)S(1)}, f32[8,16384]{1,0:T(8,128)}, u32[]{:S(2)}) copy-start(f32[8,16384]{1,0:T(8,128)} %all-reduce.9.cloned.1.call-done) | copy-start | bytes 1572868
  492.8 5.3 collective-permute-start.6
  498.9 168.1 %all-reduce.15.cloned.1.call-start = ((), (), s32[]{:S(2)}) async-start(), calls=%async_computation.3 | async-start | bytes 1048576 | tf_op jit(solution)/shard_map/psum | solution.py:84
  533.4 6.2 collective-permute-start.7
  627.2 6.5 copy-start.6
  627.2 39.8 %copy-start.3 = (f32[8,16384]{1,0:T(8,128)S(1)}, f32[8,16384]{1,0:T(8,128)}, u32[]{:S(2)}) copy-start(f32[8,16384]{1,0:T(8,128)} %all-reduce.9.cloned.1.call-done) | copy-start | bytes 1572868
  627.5 39.6 %copy-start.4 = (f32[8,16384]{1,0:T(8,128)S(1)}, f32[8,16384]{1,0:T(8,128)}, u32[]{:S(2)}) copy-start(f32[8,16384]{1,0:T(8,128)} %all-reduce.13.cloned.1.call-done) | copy-start | bytes 1572868
  627.5 5.4 collective-permute-start.8
Sparse Core Ops, SparseCore 0:
  227.9 36.0 all-reduce.8
  364.5 33.0 all-reduce.10
  499.1 33.0 all-reduce.12
  633.9 33.0 all-reduce.14
where the time goes:
time: 688 us; the launch traced here: 679 us
  matrix products  337 us (49%)
  waiting for transfers between devices  157 us (23%)
  other arithmetic  102 us (15%)
  local copies, waits for them, and re-layouts  43.6 us (6%)
  starting transfers between devices  23.2 us (3%)
  between operations  15.3 us (2%)
    dot_general x4, matrix products, pair_terms(): jnp.einsum('gab,qgb->gqa', tiles, jnp.take(extended, cols_here, axis=1),...  191 us
    psum x4, waiting for transfers between devices, apply_kernel(): total = lax.psum(own_terms, ('pairs', 'sub'))  134 us
    dot_general x4, matrix products, pair_terms(): jnp.einsum('gab,qga->gqb', tiles, jnp.take(extended, rows_here, axis=1),...  124 us
    dynamic_update_slice x24, other arithmetic, on_device(): lax.map(build_tiles, (rows_here.reshape(turns, group), cols_here.reshape(...  56.5 us
    reduce_sum x24, other arithmetic, wendland(): dist = jnp.sqrt(jnp.sum(diff * diff, axis=0))  27.1 us
    ppermute x9, waiting for transfers between devices, shifted(): lax.ppermute(value, axis, [(source, source + steps) for source in range(l...  22.7 us
    ppermute x9, starting transfers between devices, shifted(): lax.ppermute(value, axis, [(source, source + steps) for source in range(l...  22.4 us
    gather x24, local copies, waits for them, and re-layouts, build_tiles(): jnp.take(coords_ext, row_ids, axis=1)  13.8 us
  transfers between devices with their start and end apart: 13, of which 12 were waited for; matrix products, arithmetic and copies ran while one was open for 18% of the time, Pallas kernels for 0%

commit v1 on v0

v1 whole, which is shorter than its diff:
```python
import functools

import jax
import jax.numpy as jnp
from jax import lax
from jax.experimental import pallas as pl
from jax.experimental.pallas import tpu as pltpu
from jax.sharding import PartitionSpec as P

PTS_BLK = 256
REACH = 8
DEG = 4
HALO = REACH - 1
PROBES = 8

kernel_scale = 0.1
spectrum_center = 1.0
spectrum_half = 2.0

MESH = pl.DeviceIdType.MESH


def rounded(value):
    return value.astype(jnp.bfloat16).astype(jnp.float32)


def pieces(value):
    first = rounded(value)
    second = rounded(value - first)
    return first, second, rounded(value - first - second)


def stacked(value):
    high = rounded(value)
    return jnp.concatenate([high, value - high], 0).astype(jnp.bfloat16)


def kernel(
    layout,
    coords_ref,
    probes_ref,
    noise_ref,
    list_ref,
    count_ref,
    coeffs_ref,
    out_ref,
    pts,
    vec_a,
    vec_b,
    acc,
    arrived,
    keys,
    weights,
    tile_hi,
    tile_lo,
    pts_send,
    pts_recv,
    halo_send,
    halo_recv,
    term_send,
    term_recv,
    key_send,
    key_recv,
    out_send,
    out_recv,
):
    blocks, pairs, sub, split_sub, blocks_here = layout
    width = sub if split_sub else 1
    chain = pairs * width
    own = blocks_here // chain
    own_pts = own * PTS_BLK
    rim_pts = HALO * PTS_BLK
    window = REACH * PTS_BLK
    g = lax.axis_index("groups")
    b = lax.axis_index("blocks")
    p = lax.axis_index("pairs")
    s = lax.axis_index("sub")

    def position(b, p, s):
        lane = s + lax.rem(p, 2) * (sub - 1 - 2 * s) if split_sub else 0
        along = p * width + lane
        return along + lax.rem(b, 2) * (chain - 1 - 2 * along)

    def device(rank):
        at_b = lax.div(rank, chain)
        q = lax.rem(rank, chain)
        along = q + lax.rem(at_b, 2) * (chain - 1 - 2 * q)
        at_p = lax.div(along, width)
        lane = lax.rem(along, width)
        at_s = lane + lax.rem(at_p, 2) * (sub - 1 - 2 * lane) if split_sub else s
        return (g, at_b, at_p, at_s)

    q = position(b, p, s)
    rank = b * chain + q
    has_next = rank < blocks * chain - 1
    has_prev = rank > 0
    following = device(jnp.minimum(rank + 1, blocks * chain - 1))
    preceding = device(jnp.maximum(rank - 1, 0))
    member = p * sub + s
    members = pairs * sub

    def other(step):
        there = lax.rem(member + step, members)
        return (g, b, lax.div(there, sub), lax.rem(there, sub))

    here = pl.ds(pl.multiple_of(q * own_pts, PTS_BLK), own_pts)
    pts[...] = jnp.zeros_like(pts)
    pts[0:3, 0:own_pts] = coords_ref[:, here]
    vec_a[:, 0:own_pts] = probes_ref[:, here]
    vec_a[:, own_pts:] = jnp.zeros((PROBES, rim_pts), jnp.float32)
    vec_b[:, own_pts:] = jnp.zeros((PROBES, rim_pts), jnp.float32)
    cap = list_ref.shape[1]
    slot_ids = lax.broadcasted_iota(jnp.int32, (1, cap), 1)
    first_of = list_ref[0:1, :]
    key = (first_of - b * blocks_here) * REACH + list_ref[1:2, :] - first_of
    my_keys = keys.at[member]
    my_keys[...] = jnp.full(my_keys.shape, -1, jnp.int32)
    my_keys[0:1, 0:cap] = jnp.where(slot_ids < count_ref[0], key, -1)

    barrier = pltpu.get_barrier_semaphore()
    cross_next = (q == chain - 1) & has_next
    cross_prev = (q == 0) & has_prev
    for step in range(1, members):
        pl.semaphore_signal(barrier, inc=1, device_id=other(step), device_id_type=MESH)

    @pl.when(cross_next)
    def _():
        pl.semaphore_signal(barrier, inc=1, device_id=following, device_id_type=MESH)

    @pl.when(cross_prev)
    def _():
        pl.semaphore_signal(barrier, inc=1, device_id=preceding, device_id_type=MESH)

    greeted = members - 1 + cross_next.astype(jnp.int32) + cross_prev.astype(jnp.int32)
    pl.semaphore_wait(barrier, greeted)

    def rim_copy(buffer, send, recv):
        return pltpu.make_async_remote_copy(
            src_ref=buffer.at[:, pl.ds(0, rim_pts)],
            dst_ref=buffer.at[:, pl.ds(own_pts, rim_pts)],
            send_sem=send,
            recv_sem=recv,
            device_id=preceding,
            device_id_type=MESH,
        )

    def term_copy(order):
        return pltpu.make_async_remote_copy(
            src_ref=acc.at[:, pl.ds(own_pts, rim_pts)],
            dst_ref=arrived,
            send_sem=term_send.at[order],
            recv_sem=term_recv.at[order],
            device_id=following,
            device_id_type=MESH,
        )

    pts_copy = rim_copy(pts, pts_send, pts_recv)
    halo_copies = [
        rim_copy((vec_a, vec_b)[k % 2], halo_send.at[k], halo_recv.at[k]) for k in range(DEG)
    ]
    term_copies = [term_copy(k) for k in range(DEG)]
    key_copies = [
        pltpu.make_async_remote_copy(
            src_ref=my_keys,
            dst_ref=my_keys,
            send_sem=key_send.at[step],
            recv_sem=key_recv.at[step],
            device_id=other(step),
            device_id_type=MESH,
        )
        for step in range(1, members)
    ]

    @pl.when(has_prev)
    def _():
        pts_copy.start()
        halo_copies[0].start()

    for copy in key_copies:
        copy.start()

    row8 = lax.broadcasted_iota(jnp.int32, (8, 1), 0)

    def build_row(i, carry):
        start = pl.multiple_of(i * PTS_BLK, PTS_BLK)
        block_id = b * blocks_here + q * own + i
        middle = block_id.astype(jnp.float32) * 0.5 + 2.0
        centre = jnp.where(row8 == 0, middle, jnp.where(row8 < 3, 1.5, 0.0))
        local = pts[:, pl.ds(start, window)] - centre
        norm = jnp.sum(local * local, axis=0, keepdims=True)
        b0, b1, b2 = pieces(jnp.where(row8 == 4, norm, local))
        right = jnp.concatenate(
            [
                jnp.where(row8 == 3, 1.0, b0),
                jnp.where(row8 == 3, 1.0, b1),
                jnp.where(row8 < 3, b0, jnp.where(row8 == 3, 1.0, b2)),
                b1,
                b2,
                b0,
            ],
            0,
        ).astype(jnp.bfloat16)
        a0, a1, a2 = pieces(
            jnp.where(row8 == 3, norm[:, :PTS_BLK], -2.0 * local[:, :PTS_BLK])
        )
        left = jnp.concatenate(
            [
                jnp.where(row8 == 4, 1.0, a0),
                jnp.where(row8 < 3, a0, jnp.where(row8 == 4, 1.0, a1)),
                jnp.where(row8 < 3, a1, jnp.where(row8 == 4, 1.0, a2)),
                jnp.where(row8 < 3, a1, 0.0),
                jnp.where(row8 < 3, a0, 0.0),
                jnp.where(row8 < 3, a2, 0.0),
            ],
            0,
        )
        left = left.T.astype(jnp.bfloat16)
        for d in range(REACH):
            columns = slice(d * PTS_BLK, (d + 1) * PTS_BLK)
            square = jnp.dot(left, right[:, columns], preferred_element_type=jnp.float32)
            square = jnp.maximum(square, 1e-12)
            inside = jnp.maximum(1.0 - square * lax.rsqrt(square), 0.0)
            inside2 = inside * inside
            tile = (inside2 * inside2) * (5.0 * kernel_scale - 4.0 * kernel_scale * inside)
            high = tile.astype(jnp.bfloat16)
            tile_hi[i, :, columns] = high
            tile_lo[i, :, columns] = (tile - high.astype(jnp.float32)).astype(jnp.bfloat16)
        return carry

    inner = own - HALO
    lax.fori_loop(0, inner, build_row, 0)

    @pl.when(has_next)
    def _():
        pts_copy.wait_recv()

    lax.fori_loop(inner, own, build_row, 0)

    for copy in key_copies:
        copy.wait_recv()
    own_rows = lax.broadcasted_iota(jnp.int32, (own, 1), 0)
    for d in range(REACH):
        ids = (q * own + own_rows) * REACH + d
        count = jnp.zeros((own, 1), jnp.float32)
        for m in range(members):
            same = jnp.where(keys[m, 0:1, :] == ids, 1.0, 0.0)
            count = count + jnp.sum(same, axis=1, keepdims=True)
        weights[:, d * PTS_BLK : (d + 1) * PTS_BLK] = jnp.broadcast_to(count, (own, PTS_BLK))

    off_diagonal = lax.broadcasted_iota(jnp.int32, (1, window), 1) >= PTS_BLK

    def apply_rows(current):
        def body(i, carry):
            start = pl.multiple_of(i * PTS_BLK, PTS_BLK)
            weight = weights[pl.ds(i, 1), :]
            reach = pl.ds(start, window)
            block = pl.ds(start, PTS_BLK)
            seen = stacked(current[:, reach] * weight)
            mine = stacked(current[:, block])
            by_last = (((1,), (1,)), ((), ()))
            fwd = lax.dot_general(seen, tile_hi[i], by_last, preferred_element_type=jnp.float32)
            fwd += lax.dot_general(seen, tile_lo[i], by_last, preferred_element_type=jnp.float32)
            bwd = jnp.dot(mine, tile_hi[i], preferred_element_type=jnp.float32)
            bwd += jnp.dot(mine, tile_lo[i], preferred_element_type=jnp.float32)
            back = (bwd[:PROBES] + bwd[PROBES:]) * jnp.where(off_diagonal, weight, 0.0)
            acc[:, reach] += back
            acc[:, block] += fwd[:PROBES] + fwd[PROBES:]
            return carry

        return body

    early = (inner + 1) // 2
    for k in range(DEG):
        current = (vec_a, vec_b)[k % 2]
        before = (vec_b, vec_a)[k % 2]
        body = apply_rows(current)
        acc[...] = jnp.zeros_like(acc)
        lax.fori_loop(0, early, body, 0)

        @pl.when(has_next)
        def _():
            halo_copies[k].wait_recv()

        lax.fori_loop(inner, own, body, 0)

        @pl.when(has_next)
        def _():
            term_copies[k].start()

        lax.fori_loop(early, inner, body, 0)

        @pl.when(has_prev)
        def _():
            halo_copies[k].wait_send()
            term_copies[k].wait_recv()
            acc[:, 0:rim_pts] += arrived[...]

        def advance(lo, hi):
            at = pl.ds(pl.multiple_of(q * own_pts + lo, PTS_BLK), hi - lo)
            value = current[:, lo:hi]
            moved = noise_ref[:, at] * value + acc[:, lo:hi] - spectrum_center * value
            if k == 0:
                fresh = moved / spectrum_half
                out_ref[:, at] = coeffs_ref[0] * value + coeffs_ref[1] * fresh
            else:
                fresh = moved * (2.0 / spectrum_half) - before[:, lo:hi]
                out_ref[:, at] = out_ref[:, at] + coeffs_ref[k + 1] * fresh
            if k < DEG - 1:
                before[:, lo:hi] = fresh

        advance(0, rim_pts)
        if k < DEG - 1:

            @pl.when(has_prev)
            def _():
                halo_copies[k + 1].start()

        advance(rim_pts, own_pts)

        @pl.when(has_next)
        def _():
            term_copies[k].wait_send()

    @pl.when(has_prev)
    def _():
        pts_copy.wait_send()

    for copy in key_copies:
        copy.wait_send()

    def out_copy(at_p, sem, device_id):
        at_q = position(b, at_p, s)
        part = out_ref.at[:, pl.ds(pl.multiple_of(at_q * own_pts, PTS_BLK), own_pts)]
        return pltpu.make_async_remote_copy(
            src_ref=part,
            dst_ref=part,
            send_sem=out_send.at[sem],
            recv_sem=out_recv.at[sem],
            device_id=device_id,
            device_id_type=MESH,
        )

    across = [out_copy(p, step, (g, b, lax.rem(p + step, pairs), s)) for step in range(1, pairs)]
    for copy in across:
        copy.start()
    inside = []
    if split_sub:
        for step in range(pairs):
            if step > 0:
                across[step - 1].wait_recv()
            source = lax.rem(p + pairs - step, pairs)
            for turn in range(1, sub):
                sem = pairs + step * sub + turn
                copy = out_copy(source, sem, (g, b, p, lax.rem(s + turn, sub)))
                copy.start()
                inside.append(copy)
    else:
        for copy in across:
            copy.wait_recv()
    for copy in inside:
        copy.wait_recv()
    for copy in across + inside:
        copy.wait_send()


def on_device(layout, coords, probes, noise, pair_list, pair_count, coeffs):
    blocks, pairs, sub, split_sub, blocks_here = layout
    own = blocks_here // (pairs * (sub if split_sub else 1))
    members = pairs * sub
    own_pts = own * PTS_BLK
    ext_pts = own_pts + HALO * PTS_BLK
    window = REACH * PTS_BLK
    key_lanes = -(-pair_list.shape[1] // 128) * 128
    dma = pltpu.SemaphoreType.DMA
    vmem = pl.BlockSpec(memory_space=pltpu.VMEM)
    smem = pl.BlockSpec(memory_space=pltpu.SMEM)
    return pl.pallas_call(
        functools.partial(kernel, layout),
        out_shape=jax.ShapeDtypeStruct(probes.shape, jnp.float32),
        in_specs=[vmem, vmem, vmem, vmem, smem, smem],
        out_specs=vmem,
        scratch_shapes=[
            pltpu.VMEM((8, ext_pts), jnp.float32),
            pltpu.VMEM((PROBES, ext_pts), jnp.float32),
            pltpu.VMEM((PROBES, ext_pts), jnp.float32),
            pltpu.VMEM((PROBES, ext_pts), jnp.float32),
            pltpu.VMEM((PROBES, HALO * PTS_BLK), jnp.float32),
            pltpu.VMEM((members, 8, key_lanes), jnp.int32),
            pltpu.VMEM((own, window), jnp.float32),
            pltpu.VMEM((own, PTS_BLK, window), jnp.bfloat16),
            pltpu.VMEM((own, PTS_BLK, window), jnp.bfloat16),
            dma,
            dma,
            dma((DEG,)),
            dma((DEG,)),
            dma((DEG,)),
            dma((DEG,)),
            dma((members,)),
            dma((members,)),
            dma((pairs + members,)),
            dma((pairs + members,)),
        ],
        compiler_params=pltpu.CompilerParams(
            collective_id=0, has_side_effects=True, vmem_limit_bytes=56 * 1024 * 1024
        ),
    )(coords, probes, noise.reshape(1, -1), pair_list, pair_count, coeffs)


def solution(mesh):
    blocks, pairs, sub = (mesh.shape[axis] for axis in ("blocks", "pairs", "sub"))

    def program(coords, *rest):
        total = coords.shape[1] // PTS_BLK
        blocks_here = total // (mesh.shape["groups"] * blocks)
        split_sub = blocks_here // (pairs * sub) >= REACH
        layout = (blocks, pairs, sub, split_sub, blocks_here)
        return jax.shard_map(
            functools.partial(on_device, layout),
            mesh=mesh,
            in_specs=(
                P(None, ("groups", "blocks")),
                P(None, ("groups", "blocks")),
                P(("groups", "blocks")),
                P(None, ("groups", "blocks", "pairs", "sub")),
                P(("groups", "blocks", "pairs", "sub")),
                P("groups"),
            ),
            out_specs=P(None, ("groups", "blocks")),
            check_vma=False,
        )(coords, *rest)

    return program
```

time: 688 us -> 94.2 us (0.14); the launches traced: 679 us -> 94 us
  matrix products: 337 us -> 0 us
  waiting for transfers between devices: 157 us -> 0 us
  other arithmetic: 102 us -> 0 us
  Pallas kernels: 0 us -> 91.5 us
  local copies, waits for them, and re-layouts: 43.6 us -> 1.87 us
  starting transfers between devices: 23.2 us -> 0 us
  between operations: 15.3 us -> 0.66 us
    dot_general x16 -> x0, matrix products: 337 us -> none  [the longest x4 191 us: pair_terms(): jnp.einsum('gab,qgb->gqa', tiles, jnp.take(extended, cols_here, axis=1),...]
    psum x4 -> x0, waiting for transfers between devices: 134 us -> none  [apply_kernel(): total = lax.psum(own_terms, ('pairs', 'sub'))]
    pallas_call x0 -> x1, Pallas kernels: none -> 91.5 us  [on_device(): pl.pallas_call(functools.partial(kernel, layout), out_shape=jax.ShapeDtyp...]
    dynamic_update_slice x24 -> x0, other arithmetic: 56.5 us -> none  [on_device(): lax.map(build_tiles, (rows_here.reshape(turns, group), cols_here.reshape(...]
    gather x56 -> x0, local copies, waits for them, and re-layouts: 39.4 us -> none  [the longest x24 13.8 us: build_tiles(): jnp.take(coords_ext, row_ids, axis=1)]
    reduce_sum x24 -> x0, other arithmetic: 27.1 us -> none  [wendland(): dist = jnp.sqrt(jnp.sum(diff * diff, axis=0))]
    ppermute x9 -> x0, waiting for transfers between devices: 22.7 us -> none  [shifted(): lax.ppermute(value, axis, [(source, source + steps) for source in range(l...]
    ppermute x9 -> x0, starting transfers between devices: 22.4 us -> none  [shifted(): lax.ppermute(value, axis, [(source, source + steps) for source in range(l...]
  transfers between devices with their start and end apart: 13 -> 0, of which waited for: 12 -> 0; matrix products, arithmetic and copies ran while one was open for 18% -> 0% of each run, Pallas kernels for 0% -> 0%
where the time goes in v1:
time: 94.2 us; the launch traced here: 94 us
  Pallas kernels  91.5 us (97%)
  local copies, waits for them, and re-layouts  1.87 us (2%)
    pallas_call x1, Pallas kernels, on_device(): pl.pallas_call(functools.partial(kernel, layout), out_shape=jax.ShapeDtyp...  91.5 us

profile of v1, /device:TPU:0, one launch (start us, length us, event | category | flops | bytes accessed | tf_op | source)
XLA Modules:
  0.0 94.0 jit_solution(7606826059123328833)
XLA Ops:
  0.7 91.5 %shard_map.64 = f32[8,16384]{1,0:T(8,128)} custom-call(f32[3,16384]{1,0:T(4,128)} %coords_ref.1, f32[8,16384]{1,0:T(8,128)} %probes_ref.1, f32[1,16384]{1,0:T(1,128)} %bitcast.1, s32[2,192]{1,0:T(2,128)} %list_ref.1, s32[1]{0:T(128)S(6)} %copy.8.count_ref, f32[5]{0:T(128)} %coeffs_ref.1), custom_call_target="tpu_custom_call" | custom-call | tf_op jit(solution)/shard_map/pallas_call | solution.py:377
  92.1 1.9 %copy.9 = f32[8,16384]{1,0:T(8,128)} copy(f32[8,16384]{1,0:T(8,128)} %shard_map.64) | data formatting | bytes 1048576

commit v2 on v1

--- a/solution.py
+++ b/solution.py
@@ -18,6 +18,10 @@
 spectrum_half = 2.0
 
 MESH = pl.DeviceIdType.MESH
+
+TILE_UNIT = 2.0**20
+STRETCH = (4.0 * kernel_scale * TILE_UNIT) ** 0.2
+TOP = 240.0
 
 
 def rounded(value):
@@ -186,7 +190,7 @@
         block_id = b * blocks_here + q * own + i
         middle = block_id.astype(jnp.float32) * 0.5 + 2.0
         centre = jnp.where(row8 == 0, middle, jnp.where(row8 < 3, 1.5, 0.0))
-        local = pts[:, pl.ds(start, window)] - centre
+        local = (pts[:, pl.ds(start, window)] - centre) * STRETCH
         norm = jnp.sum(local * local, axis=0, keepdims=True)
         b0, b1, b2 = pieces(jnp.where(row8 == 4, norm, local))
         right = jnp.concatenate(
@@ -218,13 +222,13 @@
         for d in range(REACH):
             columns = slice(d * PTS_BLK, (d + 1) * PTS_BLK)
             square = jnp.dot(left, right[:, columns], preferred_element_type=jnp.float32)
-            square = jnp.maximum(square, 1e-12)
-            inside = jnp.maximum(1.0 - square * lax.rsqrt(square), 0.0)
+            square = jnp.maximum(square, 1e-10)
+            inside = jnp.maximum(STRETCH - square * lax.rsqrt(square), 0.0)
             inside2 = inside * inside
-            tile = (inside2 * inside2) * (5.0 * kernel_scale - 4.0 * kernel_scale * inside)
+            tile = (inside2 * inside2) * (1.25 * STRETCH - inside)
             high = tile.astype(jnp.bfloat16)
             tile_hi[i, :, columns] = high
-            tile_lo[i, :, columns] = (tile - high.astype(jnp.float32)).astype(jnp.bfloat16)
+            tile_lo[i, :, columns] = (tile - high.astype(jnp.float32)).astype(jnp.float8_e4m3fn)
         return carry
 
     inner = own - HALO
@@ -247,33 +251,49 @@
             count = count + jnp.sum(same, axis=1, keepdims=True)
         weights[:, d * PTS_BLK : (d + 1) * PTS_BLK] = jnp.broadcast_to(count, (own, PTS_BLK))
 
-    off_diagonal = lax.broadcasted_iota(jnp.int32, (1, window), 1) >= PTS_BLK
-
-    def apply_rows(current):
+    heaviest = jnp.max(weights[...], axis=(0, 1), keepdims=True)
+    heaviest = jnp.maximum(heaviest, 1.0)
+    by_last = (((1,), (1,)), ((), ()))
+
+    def apply_rows(current, peak):
+        shrink = TOP / jnp.maximum(peak, 1e-30)
+        grow = peak * (1.0 / TOP)
+        shrink_seen = shrink / heaviest
+        grow_seen = grow * heaviest
+
         def body(i, carry):
             start = pl.multiple_of(i * PTS_BLK, PTS_BLK)
             weight = weights[pl.ds(i, 1), :]
             reach = pl.ds(start, window)
             block = pl.ds(start, PTS_BLK)
-            seen = stacked(current[:, reach] * weight)
-            mine = stacked(current[:, block])
-            by_last = (((1,), (1,)), ((), ()))
-            fwd = lax.dot_general(seen, tile_hi[i], by_last, preferred_element_type=jnp.float32)
-            fwd += lax.dot_general(seen, tile_lo[i], by_last, preferred_element_type=jnp.float32)
-            bwd = jnp.dot(mine, tile_hi[i], preferred_element_type=jnp.float32)
-            bwd += jnp.dot(mine, tile_lo[i], preferred_element_type=jnp.float32)
-            back = (bwd[:PROBES] + bwd[PROBES:]) * jnp.where(off_diagonal, weight, 0.0)
-            acc[:, reach] += back
-            acc[:, block] += fwd[:PROBES] + fwd[PROBES:]
+            beyond = pl.ds(pl.multiple_of(start + PTS_BLK, PTS_BLK), rim_pts)
+            seen = current[:, beyond] * weight[:, PTS_BLK:]
+            mine = current[:, block]
+            seen_low = (seen * shrink_seen).astype(jnp.float8_e4m3fn)
+            mine_low = (mine * shrink).astype(jnp.float8_e4m3fn)
+            fwd = lax.dot_general(
+                stacked(seen), tile_hi[i, :, PTS_BLK:], by_last, preferred_element_type=jnp.float32
+            )
+            fwd_low = lax.dot_general(
+                seen_low, tile_lo[i, :, PTS_BLK:], by_last, preferred_element_type=jnp.float32
+            )
+            bwd = jnp.dot(stacked(mine), tile_hi[i], preferred_element_type=jnp.float32)
+            bwd_low = jnp.dot(mine_low, tile_lo[i], preferred_element_type=jnp.float32)
+            acc[:, reach] += (bwd[:PROBES] + bwd[PROBES:] + bwd_low * grow) * weight
+            acc[:, block] += fwd[:PROBES] + fwd[PROBES:] + fwd_low * grow_seen
             return carry
 
         return body
+
+    def peak_of(value):
+        return jnp.max(jnp.abs(value), axis=(0, 1), keepdims=True)
 
     early = (inner + 1) // 2
     for k in range(DEG):
         current = (vec_a, vec_b)[k % 2]
         before = (vec_b, vec_a)[k % 2]
-        body = apply_rows(current)
+        peak = peak_of(current[:, 0:own_pts])
+        body = apply_rows(current, peak)
         acc[...] = jnp.zeros_like(acc)
         lax.fori_loop(0, early, body, 0)
 
@@ -281,7 +301,9 @@
         def _():
             halo_copies[k].wait_recv()
 
-        lax.fori_loop(inner, own, body, 0)
+        peak = jnp.maximum(peak, peak_of(current[:, own_pts:]))
+        acc_body = apply_rows(current, peak)
+        lax.fori_loop(inner, own, acc_body, 0)
 
         @pl.when(has_next)
         def _():
@@ -298,7 +320,7 @@
         def advance(lo, hi):
             at = pl.ds(pl.multiple_of(q * own_pts + lo, PTS_BLK), hi - lo)
             value = current[:, lo:hi]
-            moved = noise_ref[:, at] * value + acc[:, lo:hi] - spectrum_center * value
+            moved = noise_ref[:, at] * value + acc[:, lo:hi] * (1.0 / TILE_UNIT) - spectrum_center * value
             if k == 0:
                 fresh = moved / spectrum_half
                 out_ref[:, at] = coeffs_ref[0] * value + coeffs_ref[1] * fresh
@@ -388,7 +410,7 @@
             pltpu.VMEM((members, 8, key_lanes), jnp.int32),
             pltpu.VMEM((own, window), jnp.float32),
             pltpu.VMEM((own, PTS_BLK, window), jnp.bfloat16),
-            pltpu.VMEM((own, PTS_BLK, window), jnp.bfloat16),
+            pltpu.VMEM((own, PTS_BLK, window), jnp.float8_e4m3fn),
             dma,
             dma,
             dma((DEG,)),
@@ -401,7 +423,7 @@
             dma((pairs + members,)),
         ],
         compiler_params=pltpu.CompilerParams(
-            collective_id=0, has_side_effects=True, vmem_limit_bytes=56 * 1024 * 1024
+            collective_id=0, has_side_effects=True, vmem_limit_bytes=48 * 1024 * 1024
         ),
     )(coords, probes, noise.reshape(1, -1), pair_list, pair_count, coeffs)
 

time: 94.2 us -> 79.3 us (0.84)
  Pallas kernels: 91.5 us -> 74 us
  local copies, waits for them, and re-layouts: 1.87 us -> 4.27 us
    pallas_call x1, Pallas kernels: 91.5 us -> 74 us  [on_device(): pl.pallas_call(functools.partial(kernel, layout), out_shape=jax.ShapeDtyp...]
    unnamed x1 -> x11, local copies, waits for them, and re-layouts: 1.87 us -> 4.27 us
where the time goes in v2:
time: 79.3 us; the launch traced here: 79 us
  Pallas kernels  74 us (93%)
  local copies, waits for them, and re-layouts  4.27 us (5%)
    pallas_call x1, Pallas kernels, on_device(): pl.pallas_call(functools.partial(kernel, layout), out_shape=jax.ShapeDtyp...  74 us
    unnamed x11, local copies, waits for them, and re-layouts  4.27 us

profile of v2, /device:TPU:0, one launch (start us, length us, event | category | flops | bytes accessed | tf_op | source)
XLA Modules:
  0.0 79.0 jit_solution(8733730648719508247)
XLA Ops:
  0.0 0.0 copy-start.3
  0.7 0.0 copy-start.4
  0.7 0.0 copy-done.3
  0.7 0.6 copy-done.4
  1.3 0.0 copy-start
  1.3 1.0 %copy-done = f32[8,16384]{1,0:T(8,128)S(1)} copy-done((f32[8,16384]{1,0:T(8,128)S(1)}, f32[8,16384]{1,0:T(8,128)}, u32[]{:S(2)}) %copy-start) | copy-done | bytes 524312
  2.4 0.0 copy-start.1
  2.4 0.9 %copy-done.1 = f32[3,16384]{1,0:T(4,128)S(1)} copy-done((f32[3,16384]{1,0:T(4,128)S(1)}, f32[3,16384]{1,0:T(4,128)}, u32[]{:S(2)}) %copy-start.1) | copy-done | bytes 196632
  3.3 0.0 copy-start.2
  3.3 0.8 %copy-done.2 = f32[16384]{0:T(1024)S(1)} copy-done((f32[16384]{0:T(1024)S(1)}, f32[16384]{0:T(1024)}, u32[]{:S(2)}) %copy-start.2) | copy-done | bytes 65560
  4.2 74.0 %shard_map.64 = f32[8,16384]{1,0:T(8,128)S(1)} custom-call(f32[3,16384]{1,0:T(4,128)S(1)} %copy-done.1, f32[8,16384]{1,0:T(8,128)S(1)} %copy-done, f32[1,16384]{1,0:T(1,128)S(1)} %bitcast.1, s32[2,192]{1,0:T(2,128)S(1)} %copy-done.3, s32[1]{0:T(128)S(6)} %copy.8.count_ref, f32[5]{0:T(128)S(1)} %copy-done.4), custom_call_target="tpu_custom_call" | custom-call | tf_op jit(solution)/shard_map/pallas_call | solution.py:399
  78.2 0.8 %copy.9 = f32[8,16384]{1,0:T(8,128)} copy(f32[8,16384]{1,0:T(8,128)S(1)} %shard_map.64) | data formatting | bytes 1048576
Async XLA Ops:
  0.0 0.7 copy-start.3
  0.7 0.7 copy-start.4
  1.3 1.0 %copy-start = (f32[8,16384]{1,0:T(8,128)S(1)}, f32[8,16384]{1,0:T(8,128)}, u32[]{:S(2)}) copy-start(f32[8,16384]{1,0:T(8,128)} %probes_ref.1) | copy-start | bytes 1572868
  2.4 0.9 %copy-start.1 = (f32[3,16384]{1,0:T(4,128)S(1)}, f32[3,16384]{1,0:T(4,128)}, u32[]{:S(2)}) copy-start(f32[3,16384]{1,0:T(4,128)} %coords_ref.1) | copy-start | bytes 589828
  3.3 0.8 %copy-start.2 = (f32[16384]{0:T(1024)S(1)}, f32[16384]{0:T(1024)}, u32[]{:S(2)}) copy-start(f32[16384]{0:T(1024)} %param.8) | copy-start | bytes 196612

commit v3 on v2

--- a/solution.py
+++ b/solution.py
@@ -1,4 +1,5 @@
 import functools
+import math
 
 import jax
 import jax.numpy as jnp
@@ -57,6 +58,8 @@
     weights,
     tile_hi,
     tile_lo,
+    turned_hi,
+    turned_lo,
     pts_send,
     pts_recv,
     halo_send,
@@ -228,7 +231,12 @@
             tile = (inside2 * inside2) * (1.25 * STRETCH - inside)
             high = tile.astype(jnp.bfloat16)
             tile_hi[i, :, columns] = high
-            tile_lo[i, :, columns] = (tile - high.astype(jnp.float32)).astype(jnp.float8_e4m3fn)
+            low = tile - high.astype(jnp.float32)
+            tile_lo[i, :, columns] = low.astype(jnp.float8_e4m3fn)
+            if d > 0:
+                rows = slice((d - 1) * PTS_BLK, d * PTS_BLK)
+                turned_hi[i, rows, :] = high.T
+                turned_lo[i, rows, :] = low.astype(jnp.bfloat16).T.astype(jnp.float8_e4m3fn)
         return carry
 
     inner = own - HALO
@@ -253,7 +261,7 @@
 
     heaviest = jnp.max(weights[...], axis=(0, 1), keepdims=True)
     heaviest = jnp.maximum(heaviest, 1.0)
-    by_last = (((1,), (1,)), ((), ()))
+    group = math.gcd(own, 4)
 
     def apply_rows(current, peak):
         shrink = TOP / jnp.maximum(peak, 1e-30)
@@ -261,26 +269,29 @@
         shrink_seen = shrink / heaviest
         grow_seen = grow * heaviest
 
-        def body(i, carry):
-            start = pl.multiple_of(i * PTS_BLK, PTS_BLK)
-            weight = weights[pl.ds(i, 1), :]
-            reach = pl.ds(start, window)
-            block = pl.ds(start, PTS_BLK)
-            beyond = pl.ds(pl.multiple_of(start + PTS_BLK, PTS_BLK), rim_pts)
-            seen = current[:, beyond] * weight[:, PTS_BLK:]
-            mine = current[:, block]
-            seen_low = (seen * shrink_seen).astype(jnp.float8_e4m3fn)
-            mine_low = (mine * shrink).astype(jnp.float8_e4m3fn)
-            fwd = lax.dot_general(
-                stacked(seen), tile_hi[i, :, PTS_BLK:], by_last, preferred_element_type=jnp.float32
-            )
-            fwd_low = lax.dot_general(
-                seen_low, tile_lo[i, :, PTS_BLK:], by_last, preferred_element_type=jnp.float32
-            )
-            bwd = jnp.dot(stacked(mine), tile_hi[i], preferred_element_type=jnp.float32)
-            bwd_low = jnp.dot(mine_low, tile_lo[i], preferred_element_type=jnp.float32)
-            acc[:, reach] += (bwd[:PROBES] + bwd[PROBES:] + bwd_low * grow) * weight
-            acc[:, block] += fwd[:PROBES] + fwd[PROBES:] + fwd_low * grow_seen
+        def body(turn, carry):
+            found = []
+            for step in range(group):
+                i = turn * group + step
+                start = pl.multiple_of(i * PTS_BLK, PTS_BLK)
+                weight = weights[pl.ds(i, 1), :]
+                reach = pl.ds(start, window)
+                block = pl.ds(start, PTS_BLK)
+                beyond = pl.ds(pl.multiple_of(start + PTS_BLK, PTS_BLK), rim_pts)
+                seen = current[:, beyond] * weight[:, PTS_BLK:]
+                mine = current[:, block]
+                seen_low = (seen * shrink_seen).astype(jnp.float8_e4m3fn)
+                mine_low = (mine * shrink).astype(jnp.float8_e4m3fn)
+                fwd = jnp.dot(stacked(seen), turned_hi[i], preferred_element_type=jnp.float32)
+                fwd_low = jnp.dot(seen_low, turned_lo[i], preferred_element_type=jnp.float32)
+                bwd = jnp.dot(stacked(mine), tile_hi[i], preferred_element_type=jnp.float32)
+                bwd_low = jnp.dot(mine_low, tile_lo[i], preferred_element_type=jnp.float32)
+                back = (bwd[:PROBES] + bwd[PROBES:] + bwd_low * grow) * weight
+                front = fwd[:PROBES] + fwd[PROBES:] + fwd_low * grow_seen
+                found.append((reach, block, back, front))
+            for reach, block, back, front in found:
+                acc[:, reach] += back
+                acc[:, block] += front
             return carry
 
         return body
@@ -288,34 +299,61 @@
     def peak_of(value):
         return jnp.max(jnp.abs(value), axis=(0, 1), keepdims=True)
 
-    early = (inner + 1) // 2
+    rim_turn = inner // group
+    late_turns = rim_turn // 2
+    parts = [((late_turns * group + HALO) * PTS_BLK, own_pts)]
+    middle = (late_turns * group + HALO) // 2 * PTS_BLK
+    parts += [(middle, parts[0][0]), (0, middle)]
+
+    def out_copy(at_p, part, sem, device_id):
+        lo, hi = parts[part]
+        at = position(b, at_p, s) * own_pts + lo
+        piece = out_ref.at[:, pl.ds(pl.multiple_of(at, PTS_BLK), hi - lo)]
+        return pltpu.make_async_remote_copy(
+            src_ref=piece,
+            dst_ref=piece,
+            send_sem=out_send.at[part, sem],
+            recv_sem=out_recv.at[part, sem],
+            device_id=device_id,
+            device_id_type=MESH,
+        )
+
+    across = [
+        [out_copy(p, n, step, (g, b, lax.rem(p + step, pairs), s)) for step in range(1, pairs)]
+        for n in range(len(parts))
+    ]
+
+    def to_sub(n, step):
+        source = lax.rem(p + pairs - step, pairs)
+        return [
+            out_copy(source, n, pairs + step * sub + turn, (g, b, p, lax.rem(s + turn, sub)))
+            for turn in range(1, sub if split_sub else 1)
+        ]
+
+    inside = [[to_sub(n, step) for step in range(pairs)] for n in range(len(parts))]
+
+    def send_part(n):
+        for copy in across[n] + inside[n][0]:
+            copy.start()
+
     for k in range(DEG):
         current = (vec_a, vec_b)[k % 2]
         before = (vec_b, vec_a)[k % 2]
         peak = peak_of(current[:, 0:own_pts])
         body = apply_rows(current, peak)
         acc[...] = jnp.zeros_like(acc)
-        lax.fori_loop(0, early, body, 0)
+        lax.fori_loop(late_turns, rim_turn, body, 0)
 
         @pl.when(has_next)
         def _():
             halo_copies[k].wait_recv()
 
         peak = jnp.maximum(peak, peak_of(current[:, own_pts:]))
-        acc_body = apply_rows(current, peak)
-        lax.fori_loop(inner, own, acc_body, 0)
+        lax.fori_loop(rim_turn, own // group, apply_rows(current, peak), 0)
 
         @pl.when(has_next)
         def _():
             term_copies[k].start()
-
-        lax.fori_loop(early, inner, body, 0)
-
-        @pl.when(has_prev)
-        def _():
-            halo_copies[k].wait_send()
-            term_copies[k].wait_recv()
-            acc[:, 0:rim_pts] += arrived[...]
 
         def advance(lo, hi):
             at = pl.ds(pl.multiple_of(q * own_pts + lo, PTS_BLK), hi - lo)
@@ -330,14 +368,30 @@
             if k < DEG - 1:
                 before[:, lo:hi] = fresh
 
-        advance(0, rim_pts)
+        if k == DEG - 1:
+            advance(*parts[0])
+            send_part(0)
+
+        lax.fori_loop(0, late_turns, body, 0)
+
+        @pl.when(has_prev)
+        def _():
+            halo_copies[k].wait_send()
+            term_copies[k].wait_recv()
+            acc[:, 0:rim_pts] += arrived[...]
+
         if k < DEG - 1:
+            advance(0, rim_pts)
 
             @pl.when(has_prev)
             def _():
                 halo_copies[k + 1].start()
 
-        advance(rim_pts, own_pts)
+            advance(rim_pts, own_pts)
+        else:
+            for n in range(1, len(parts)):
+                advance(*parts[n])
+                send_part(n)
 
         @pl.when(has_next)
         def _():
@@ -350,39 +404,17 @@
     for copy in key_copies:
         copy.wait_send()
 
-    def out_copy(at_p, sem, device_id):
-        at_q = position(b, at_p, s)
-        part = out_ref.at[:, pl.ds(pl.multiple_of(at_q * own_pts, PTS_BLK), own_pts)]
-        return pltpu.make_async_remote_copy(
-            src_ref=part,
-            dst_ref=part,
-            send_sem=out_send.at[sem],
-            recv_sem=out_recv.at[sem],
-            device_id=device_id,
-            device_id_type=MESH,
-        )
-
-    across = [out_copy(p, step, (g, b, lax.rem(p + step, pairs), s)) for step in range(1, pairs)]
-    for copy in across:
-        copy.start()
-    inside = []
-    if split_sub:
-        for step in range(pairs):
-            if step > 0:
-                across[step - 1].wait_recv()
-            source = lax.rem(p + pairs - step, pairs)
-            for turn in range(1, sub):
-                sem = pairs + step * sub + turn
-                copy = out_copy(source, sem, (g, b, p, lax.rem(s + turn, sub)))
+    for n in range(len(parts)):
+        for step in range(1, pairs):
+            across[n][step - 1].wait_recv()
+            for copy in inside[n][step]:
                 copy.start()
-                inside.append(copy)
-    else:
-        for copy in across:
-            copy.wait_recv()
-    for copy in inside:
-        copy.wait_recv()
-    for copy in across + inside:
-        copy.wait_send()
+    for n in range(len(parts)):
+        for copies in inside[n]:
+            for copy in copies:
+                copy.wait()
+        for copy in across[n]:
+            copy.wait_send()
 
 
 def on_device(layout, coords, probes, noise, pair_list, pair_count, coeffs):
@@ -411,6 +443,8 @@
             pltpu.VMEM((own, window), jnp.float32),
             pltpu.VMEM((own, PTS_BLK, window), jnp.bfloat16),
             pltpu.VMEM((own, PTS_BLK, window), jnp.float8_e4m3fn),
+            pltpu.VMEM((own, HALO * PTS_BLK, PTS_BLK), jnp.bfloat16),
+            pltpu.VMEM((own, HALO * PTS_BLK, PTS_BLK), jnp.float8_e4m3fn),
             dma,
             dma,
             dma((DEG,)),
@@ -419,11 +453,11 @@
             dma((DEG,)),
             dma((members,)),
             dma((members,)),
-            dma((pairs + members,)),
-            dma((pairs + members,)),
+            dma((3, pairs + members)),
+            dma((3, pairs + members)),
         ],
         compiler_params=pltpu.CompilerParams(
-            collective_id=0, has_side_effects=True, vmem_limit_bytes=48 * 1024 * 1024
+            collective_id=0, has_side_effects=True, vmem_limit_bytes=56 * 1024 * 1024
         ),
     )(coords, probes, noise.reshape(1, -1), pair_list, pair_count, coeffs)
 

time: 79.3 us -> 72.8 us (0.918)
  Pallas kernels: 74 us -> 70.1 us
  local copies, waits for them, and re-layouts: 4.27 us -> 1.87 us
    pallas_call x1, Pallas kernels: 74 us -> 70.1 us  [on_device(): pl.pallas_call(functools.partial(kernel, layout), out_shape=jax.ShapeDtyp...]
    unnamed x11 -> x1, local copies, waits for them, and re-layouts: 4.27 us -> 1.87 us
where the time goes in v3:
time: 72.8 us; the launch traced here: 72.6 us
  Pallas kernels  70.1 us (96%)
  local copies, waits for them, and re-layouts  1.87 us (3%)
    pallas_call x1, Pallas kernels, on_device(): pl.pallas_call(functools.partial(kernel, layout), out_shape=jax.ShapeDtyp...  70.1 us
    unnamed x1, local copies, waits for them, and re-layouts  1.87 us

profile of v3, /device:TPU:0, one launch (start us, length us, event | category | flops | bytes accessed | tf_op | source)
XLA Modules:
  0.0 72.6 jit_solution(13066375857741214067)
XLA Ops:
  0.7 70.1 %shard_map.64 = f32[8,16384]{1,0:T(8,128)} custom-call(f32[3,16384]{1,0:T(4,128)} %coords_ref.1, f32[8,16384]{1,0:T(8,128)} %probes_ref.1, f32[1,16384]{1,0:T(1,128)} %bitcast.1, s32[2,192]{1,0:T(2,128)} %list_ref.1, s32[1]{0:T(128)S(6)} %copy.8.count_ref, f32[5]{0:T(128)} %coeffs_ref.1), custom_call_target="tpu_custom_call" | custom-call | tf_op jit(solution)/shard_map/pallas_call | solution.py:431
  70.7 1.9 %copy.9 = f32[8,16384]{1,0:T(8,128)} copy(f32[8,16384]{1,0:T(8,128)} %shard_map.64) | data formatting | bytes 1048576

commit v4 on v3

--- a/solution.py
+++ b/solution.py
@@ -235,8 +235,11 @@
             tile_lo[i, :, columns] = low.astype(jnp.float8_e4m3fn)
             if d > 0:
                 rows = slice((d - 1) * PTS_BLK, d * PTS_BLK)
-                turned_hi[i, rows, :] = high.T
-                turned_lo[i, rows, :] = low.astype(jnp.bfloat16).T.astype(jnp.float8_e4m3fn)
+                turned = tile.T
+                high = turned.astype(jnp.bfloat16)
+                low = turned - high.astype(jnp.float32)
+                turned_hi[i, rows, :] = high
+                turned_lo[i, rows, :] = low.astype(jnp.float8_e4m3fn)
         return carry
 
     inner = own - HALO
@@ -269,38 +272,56 @@
         shrink_seen = shrink / heaviest
         grow_seen = grow * heaviest
 
-        def body(turn, carry):
-            found = []
-            for step in range(group):
-                i = turn * group + step
-                start = pl.multiple_of(i * PTS_BLK, PTS_BLK)
-                weight = weights[pl.ds(i, 1), :]
-                reach = pl.ds(start, window)
-                block = pl.ds(start, PTS_BLK)
-                beyond = pl.ds(pl.multiple_of(start + PTS_BLK, PTS_BLK), rim_pts)
-                seen = current[:, beyond] * weight[:, PTS_BLK:]
-                mine = current[:, block]
-                seen_low = (seen * shrink_seen).astype(jnp.float8_e4m3fn)
-                mine_low = (mine * shrink).astype(jnp.float8_e4m3fn)
-                fwd = jnp.dot(stacked(seen), turned_hi[i], preferred_element_type=jnp.float32)
-                fwd_low = jnp.dot(seen_low, turned_lo[i], preferred_element_type=jnp.float32)
-                bwd = jnp.dot(stacked(mine), tile_hi[i], preferred_element_type=jnp.float32)
-                bwd_low = jnp.dot(mine_low, tile_lo[i], preferred_element_type=jnp.float32)
-                back = (bwd[:PROBES] + bwd[PROBES:] + bwd_low * grow) * weight
-                front = fwd[:PROBES] + fwd[PROBES:] + fwd_low * grow_seen
-                found.append((reach, block, back, front))
+        def row_terms(i, lo, hi):
+            start = i * PTS_BLK
+            if not isinstance(i, int):
+                start = pl.multiple_of(start, PTS_BLK)
+            weight = weights[pl.ds(i, 1), :]
+            block = pl.ds(start, PTS_BLK)
+            reach = pl.ds(start + lo * PTS_BLK, (hi - lo) * PTS_BLK)
+            mine = current[:, block]
+            mine_low = (mine * shrink).astype(jnp.float8_e4m3fn)
+            met = slice(lo * PTS_BLK, hi * PTS_BLK)
+            bwd = jnp.dot(stacked(mine), tile_hi[i, :, met], preferred_element_type=jnp.float32)
+            bwd_low = jnp.dot(mine_low, tile_lo[i, :, met], preferred_element_type=jnp.float32)
+            back = (bwd[:PROBES] + bwd[PROBES:] + bwd_low * grow) * weight[:, met]
+            first = max(lo, 1)
+            if first == hi:
+                return reach, block, back, None
+            beyond = pl.ds(start + first * PTS_BLK, (hi - first) * PTS_BLK)
+            seen = current[:, beyond] * weight[:, first * PTS_BLK : hi * PTS_BLK]
+            seen_low = (seen * shrink_seen).astype(jnp.float8_e4m3fn)
+            met = slice((first - 1) * PTS_BLK, (hi - 1) * PTS_BLK)
+            fwd = jnp.dot(stacked(seen), turned_hi[i, met, :], preferred_element_type=jnp.float32)
+            fwd_low = jnp.dot(seen_low, turned_lo[i, met, :], preferred_element_type=jnp.float32)
+            front = fwd[:PROBES] + fwd[PROBES:] + fwd_low * grow_seen
+            return reach, block, back, front
+
+        def add(found):
             for reach, block, back, front in found:
                 acc[:, reach] += back
-                acc[:, block] += front
+                if front is not None:
+                    acc[:, block] += front
+
+        def body(turn, carry):
+            add([row_terms(turn * group + step, 0, REACH) for step in range(group)])
             return carry
 
-        return body
+        def near():
+            for half in range(0, REACH, group):
+                rows = range(half, half + group)
+                add([row_terms(own - REACH + row, 0, REACH - row) for row in rows])
+
+        def far():
+            add([row_terms(own - REACH + row, REACH - row, REACH) for row in range(1, 4)])
+            add([row_terms(own - REACH + row, REACH - row, REACH) for row in range(4, REACH)])
+
+        return body, near, far
 
     def peak_of(value):
         return jnp.max(jnp.abs(value), axis=(0, 1), keepdims=True)
 
-    rim_turn = inner // group
-    late_turns = rim_turn // 2
+    late_turns = (own - REACH) // group
     parts = [((late_turns * group + HALO) * PTS_BLK, own_pts)]
     middle = (late_turns * group + HALO) // 2 * PTS_BLK
     parts += [(middle, parts[0][0]), (0, middle)]
@@ -340,16 +361,17 @@
         current = (vec_a, vec_b)[k % 2]
         before = (vec_b, vec_a)[k % 2]
         peak = peak_of(current[:, 0:own_pts])
-        body = apply_rows(current, peak)
+        body, near, _ = apply_rows(current, peak)
         acc[...] = jnp.zeros_like(acc)
-        lax.fori_loop(late_turns, rim_turn, body, 0)
+        near()
 
         @pl.when(has_next)
         def _():
             halo_copies[k].wait_recv()
 
         peak = jnp.maximum(peak, peak_of(current[:, own_pts:]))
-        lax.fori_loop(rim_turn, own // group, apply_rows(current, peak), 0)
+        _, _, far = apply_rows(current, peak)
+        far()
 
         @pl.when(has_next)
         def _():

time: 72.8 us -> 68.4 us (0.940)
  Pallas kernels: 70.1 us -> 65.6 us
    pallas_call x1, Pallas kernels: 70.1 us -> 65.6 us  [on_device(): pl.pallas_call(functools.partial(kernel, layout), out_shape=jax.ShapeDtyp...]
where the time goes in v4:
time: 68.4 us; the launch traced here: 68.2 us
  Pallas kernels  65.6 us (96%)
  local copies, waits for them, and re-layouts  1.87 us (3%)
    pallas_call x1, Pallas kernels, on_device(): pl.pallas_call(functools.partial(kernel, layout), out_shape=jax.ShapeDtyp...  65.6 us
    unnamed x1, local copies, waits for them, and re-layouts  1.87 us

profile of v4, /device:TPU:0, one launch (start us, length us, event | category | flops | bytes accessed | tf_op | source)
XLA Modules:
  0.0 68.2 jit_solution(7065278402286920316)
XLA Ops:
  0.7 65.6 %shard_map.64 = f32[8,16384]{1,0:T(8,128)} custom-call(f32[3,16384]{1,0:T(4,128)} %coords_ref.1, f32[8,16384]{1,0:T(8,128)} %probes_ref.1, f32[1,16384]{1,0:T(1,128)} %bitcast.1, s32[2,192]{1,0:T(2,128)} %list_ref.1, s32[1]{0:T(128)S(6)} %copy.8.count_ref, f32[5]{0:T(128)} %coeffs_ref.1), custom_call_target="tpu_custom_call" | custom-call | tf_op jit(solution)/shard_map/pallas_call | solution.py:453
  66.3 1.9 %copy.9 = f32[8,16384]{1,0:T(8,128)} copy(f32[8,16384]{1,0:T(8,128)} %shard_map.64) | data formatting | bytes 1048576
